TPU v7x, 32 devices: a whole 2x2x4 slice. The times are simulated.
32 devices in a mesh: rep: 8 (over y, x, core), shard: 4 (over z).
Axes of the slice: x: 2, y: 2, z: 4, core: 2. Of those that a mesh axis runs over, the one named last changes fastest.
Arguments:
- grad_embed: bfloat16 [8, 4, 2048, 768], P('rep', 'shard'), may hold values from -800 to 800
- grad_proj: bfloat16 [8, 4, 768, 768], P('rep', 'shard'), may hold values from -800 to 800
- grad_norms: bfloat16 [8, 4, 4, 768], P('rep', 'shard'), may hold values from -800 to 800
- embed_master: float32 [2048, 768], P('shard'), may hold values from -0.75 to 0.75
- embed_first: float32 [2048, 768], P('shard'), may hold values from -6 to 6
- embed_second: float32 [2048, 768], P('shard'), may hold values from 0.01 to 4
- proj_master: float32 [768, 768], P('shard'), may hold values from -0.21875 to 0.21875
- proj_first: float32 [768, 768], P('shard'), may hold values from -6 to 6
- proj_second: float32 [768, 768], P('shard'), may hold values from 0.01 to 4
- norm_master: float32 [4, 768], P(None, 'shard'), may hold values from -6 to 6
- norm_first: float32 [4, 768], P(None, 'shard'), may hold values from -6 to 6
- norm_second: float32 [4, 768], P(None, 'shard'), may hold values from 0.01 to 4
Outputs:
- embed_master_new: float32 [2048, 768], P('shard')
- embed_first_new: float32 [2048, 768], P('shard')
- embed_second_new: float32 [2048, 768], P('shard')
- embed_weights: bfloat16 [2048, 768], replicated
- proj_master_new: float32 [768, 768], P('shard')
- proj_first_new: float32 [768, 768], P('shard')
- proj_second_new: float32 [768, 768], P('shard')
- proj_weights: bfloat16 [768, 768], replicated
- norm_master_new: float32 [4, 768], P(None, 'shard')
- norm_first_new: float32 [4, 768], P(None, 'shard')
- norm_second_new: float32 [4, 768], P(None, 'shard')
- norm_weights: bfloat16 [4, 768], replicated
All inputs are finite; a program needn't handle non-finite values.
Results may differ from a plain program's by a relative error of at most 0.0004.
Values may be sent and summed in bfloat16 or wider, within the bound.
A program may use at most 128 MiB of HBM per device.

v0:
```python
import jax
import jax.numpy as jnp
from jax import lax
from jax.sharding import PartitionSpec as P

beta_one = 0.9
beta_two = 0.95
adam_step = 10.0
adam_eps = 1e-08
learning_rate = 0.002
clip_rms = 1.0


def adamw(gradient, master, first, second, weight_decay):
    corr_one = 1.0 - beta_one**adam_step
    corr_two = 1.0 - beta_two**adam_step
    first_new = beta_one * first + (1.0 - beta_one) * gradient
    second_new = beta_two * second + (1.0 - beta_two) * gradient * gradient
    direction = (
        first_new / corr_one / (jnp.sqrt(second_new / corr_two) + adam_eps) + weight_decay * master
    )
    master_new = master - learning_rate * direction
    return (master_new, first_new, second_new, master_new.astype(jnp.bfloat16))


def square_sum(embed_part, proj_part, norm_part):
    return (
        jnp.sum(embed_part * embed_part)
        + jnp.sum(proj_part * proj_part)
        + jnp.sum(norm_part * norm_part)
    )


def shards(
    grad_embed,
    grad_proj,
    grad_norms,
    embed_master,
    embed_first,
    embed_second,
    proj_master,
    proj_first,
    proj_second,
    norm_master,
    norm_first,
    norm_second,
):
    embed_term = grad_embed[0, 0].astype(jnp.float32)
    proj_term = grad_proj[0, 0].astype(jnp.float32)
    norm_term = grad_norms[0, 0].astype(jnp.float32)
    embed_rows, feature_width = embed_term.shape
    proj_rows = proj_term.shape[0]
    entry_count = float(
        embed_rows * feature_width
        + proj_rows * feature_width
        + norm_term.shape[0] * norm_term.shape[1]
    )
    embed_sum, proj_sum, norm_sum = (
        lax.psum_scatter(embed_term, "shard", scatter_dimension=0, tiled=True),
        lax.psum_scatter(proj_term, "shard", scatter_dimension=0, tiled=True),
        lax.psum_scatter(norm_term, "shard", scatter_dimension=1, tiled=True),
    )
    embed_sum, proj_sum, norm_sum = lax.psum((embed_sum, proj_sum, norm_sum), "rep")
    squares = lax.psum(square_sum(embed_sum, proj_sum, norm_sum), "shard")
    rms_value = jnp.sqrt(squares / entry_count)
    clip_factor = jnp.minimum(jnp.float32(1.0), clip_rms / (rms_value + 1e-06))
    embed_out = adamw(clip_factor * embed_sum, embed_master, embed_first, embed_second, 0.01)
    proj_out = adamw(clip_factor * proj_sum, proj_master, proj_first, proj_second, 0.01)
    norm_out = adamw(clip_factor * norm_sum, norm_master, norm_first, norm_second, 0.0)
    embed_weights, proj_weights, norm_weights = (
        lax.all_gather(embed_out[3], "shard", axis=0, tiled=True),
        lax.all_gather(proj_out[3], "shard", axis=0, tiled=True),
        lax.all_gather(norm_out[3], "shard", axis=1, tiled=True),
    )
    return (
        embed_out[0],
        embed_out[1],
        embed_out[2],
        embed_weights,
        proj_out[0],
        proj_out[1],
        proj_out[2],
        proj_weights,
        norm_out[0],
        norm_out[1],
        norm_out[2],
        norm_weights,
    )


def solution(mesh):
    return jax.shard_map(
        shards,
        mesh=mesh,
        in_specs=(
            P("rep", "shard", None, None),
            P("rep", "shard", None, None),
            P("rep", "shard", None, None),
            P("shard", None),
            P("shard", None),
            P("shard", None),
            P("shard", None),
            P("shard", None),
            P("shard", None),
            P(None, "shard"),
            P(None, "shard"),
            P(None, "shard"),
        ),
        out_specs=(
            P("shard", None),
            P("shard", None),
            P("shard", None),
            P(),
            P("shard", None),
            P("shard", None),
            P("shard", None),
            P(),
            P(None, "shard"),
            P(None, "shard"),
            P(None, "shard"),
            P(),
        ),
        check_vma=False,
    )
```

profile of v0, /device:TPU:1, one launch (start us, length us, event | category | flops | bytes accessed | tf_op | source)
XLA Modules:
  0.0 386.1 jit_solution(9178136247292171849)
XLA Ops:
  7.2 0.0 reduce-scatter.8.cloned.1.call-start
  7.2 0.0 copy-start.1
  7.2 3.0 bitcast_convert_fusion.1
  10.2 0.0 reduce-scatter.8.cloned.1.call-update
  10.3 0.0 reduce-scatter.6.cloned.1.call-start
  10.3 0.0 copy-done.1
  10.3 3.1 bitcast_convert_fusion
  13.5 0.0 reduce-scatter.6.cloned.1.call-update
  13.5 0.0 reduce-scatter.10.cloned.1.call-start
  13.5 0.6 copy-done.6
  14.2 0.9 copy.26
  15.1 0.0 reduce-scatter.10.cloned.1.call-update
  15.1 0.0 all-reduce.3.cloned.1.call-start
  15.2 45.7 %reduce-scatter.8.cloned.1.call-done = f32[192,768]{1,0:T(8,128)} async-done(((f32[768,768]{1,0:T(8,128)}), f32[192,768]{1,0:T(8,128)}) %reduce-scatter.8.cloned.1.call-update) | async-done | bytes 589840 | tf_op jit(solution)/shard_map/reduce_scatter | solution.py:60
  60.9 112.8 %reduce-scatter.6.cloned.1.call-done = f32[512,768]{1,0:T(8,128)} async-done(((f32[2048,768]{1,0:T(8,128)}), f32[512,768]{1,0:T(8,128)}) %reduce-scatter.6.cloned.1.call-update) | async-done | bytes 1572880 | tf_op jit(solution)/shard_map/reduce_scatter | solution.py:59
  173.7 0.0 all-reduce.3.cloned.1.call-update
  173.7 0.0 copy-start.4
  173.7 0.0 all-gather.6.cloned.1.call-start
  173.7 22.6 %reduce-scatter.10.cloned.1.call-done = f32[192,4]{1,0:T(8,128)} async-done(((f32[768,4]{1,0:T(8,128)}), f32[192,4]{1,0:T(8,128)}) %reduce-scatter.10.cloned.1.call-update) | async-done | bytes 3088
  196.4 1.0 copy.27
  197.3 13.2 %psum.30 = f32[4,192]{1,0:T(4,128)S(1)} all-reduce(f32[4,192]{1,0:T(4,128)S(1)} %copy.27), channel_id=1, replica_groups=mesh['rep'=8,'shard'=4] {'rep'}, use_global_device_ids=true, to_apply=%region_7.0 | all-reduce | flops 768 | bytes 6144 | tf_op jit(solution)/shard_map/psum | solution.py:63
  210.5 0.6 multiply_reduce_fusion.2
  211.1 49.4 %all-reduce.3.cloned.1.call-done = (f32[512,768]{1,0:T(8,128)}, f32[192,768]{1,0:T(8,128)}) async-done(((f32[512,768]{1,0:T(8,128)}, f32[192,768]{1,0:T(8,128)}), (f32[512,768]{1,0:T(8,128)}, f32[192,768]{1,0:T(8,128)})) %all-reduce.3.cloned.1.call-update) | async-done | bytes 2162704 | tf_op jit(solution)/shard_map/psum | solution.py:63
  260.5 2.5 multiply_reduce_fusion
  263.0 0.0 copy-done.2
  263.0 0.7 multiply_reduce_fusion.1
  265.7 10.2 %psum.31 = f32[]{:T(128)} all-reduce(f32[]{:T(128)S(6)} %add.69), channel_id=1, replica_groups=mesh['rep'=8,'shard'=4] {'shard'}, use_global_device_ids=true, to_apply=%region_9.0 | all-reduce | flops 1 | bytes 8 | tf_op jit(solution)/shard_map/psum | solution.py:64
  276.6 0.0 copy-done.5
  276.6 0.0 copy-done.4
  276.6 0.0 copy-start
  276.6 2.8 fusion.4
  279.4 0.0 all-gather.6.cloned.1.call-update
  279.4 0.0 copy-start.7
  279.5 0.0 copy-start.8
  279.5 0.0 copy-start.9
  279.5 0.0 all-gather.4.cloned.1.call-start
  279.5 0.0 copy-done
  279.5 5.6 %fusion.6 = (bf16[512,768]{1,0:T(8,128)(2,1)}, f32[512,768]{1,0:T(8,128)}, f32[512,768]{1,0:T(8,128)}, f32[512,768]{1,0:T(8,128)}) fusion(f32[512,768]{1,0:T(8,128)} %param.15, f32[512,768]{1,0:T(8,128)S(1)} %copy-done, f32[]{:T(128)S(6)} %min.3, f32[512,768]{1,0:T(8,128)} %param.16, f32[512,768]{1,0:T(8,128)} %param.17), kind=kLoop, calls=%fused_computation.20 | loop fusion | flops 6684672 | bytes 11796484 | tf_op jit(solution)/shard_map/convert_element_type | solution.py:23
  285.1 0.0 all-gather.4.cloned.1.call-update
  285.1 0.0 copy-done.7
  285.1 0.0 copy-done.8
  285.2 0.6 convert_bitcast_fusion
  285.8 9.8 %all-gather = bf16[4,192,4]{1,2,0:T(4,128)(2,1)S(1)} all-gather(bf16[1,192,4]{1,2,0:T(4,128)(2,1)S(1)} %get-tuple-element.14), channel_id=1, replica_groups=mesh['rep'=8,'shard'=4] {'shard'}, dimensions={0}, use_global_device_ids=true | all-gather | bytes 7680 | tf_op jit(solution)/shard_map/all_gather | solution.py:73
  295.6 0.7 reshape.34
  296.3 13.0 %all-gather.6.cloned.1.call-done = bf16[768,768]{1,0:T(8,128)(2,1)} async-done(((bf16[192,768]{1,0:T(8,128)(2,1)}), bf16[768,768]{1,0:T(8,128)(2,1)}) %all-gather.6.cloned.1.call-update) | async-done | bytes 1179664 | tf_op jit(solution)/shard_map/all_gather | solution.py:72
  309.3 65.1 %all-gather.4.cloned.1.call-done = bf16[2048,768]{1,0:T(8,128)(2,1)} async-done(((bf16[512,768]{1,0:T(8,128)(2,1)}), bf16[2048,768]{1,0:T(8,128)(2,1)}) %all-gather.4.cloned.1.call-update) | async-done | bytes 3145744 | tf_op jit(solution)/shard_map/all_gather | solution.py:71
  374.4 3.9 copy.32
  378.2 1.0 copy.33
  (8 shorter events, 0.0 us)
Async XLA Ops:
  7.2 53.7 %reduce-scatter.8.cloned.1.call-start = ((), (), s32[]{:S(2)}) async-start(), calls=%async_computation.4 | async-start | bytes 2949120 | tf_op jit(solution)/shard_map/reduce_scatter | solution.py:60
  7.2 3.1 copy-start.1
  10.3 163.4 %reduce-scatter.6.cloned.1.call-start = ((), (), s32[]{:S(2)}) async-start(), calls=%async_computation.3 | async-start | bytes 7864320 | tf_op jit(solution)/shard_map/reduce_scatter | solution.py:59
  13.5 0.7 copy-start.6
  13.5 182.9 %reduce-scatter.10.cloned.1.call-start = ((), (), s32[]{:S(2)}) async-start(), calls=%async_computation.7 | async-start | bytes 491520
  15.1 245.4 %all-reduce.3.cloned.1.call-start = ((), (), s32[]{:S(2)}) async-start(), calls=%async_computation.8 | async-start | bytes 4325376 | tf_op jit(solution)/shard_map/psum | solution.py:63
  173.7 103.0 %copy-start.5 = (f32[192,768]{1,0:T(8,128)S(1)}, f32[192,768]{1,0:T(8,128)}, u32[]{:S(2)}) copy-start(f32[192,768]{1,0:T(8,128)} %param.19) | copy-start | bytes 1769476
  173.7 102.9 %copy-start.4 = (f32[192,768]{1,0:T(8,128)S(1)}, f32[192,768]{1,0:T(8,128)}, u32[]{:S(2)}) copy-start(f32[192,768]{1,0:T(8,128)} %param.18) | copy-start | bytes 1769476
  173.7 135.6 %all-gather.6.cloned.1.call-start = ((), (), s32[]{:S(2)}) async-start(), calls=%async_computation.6 | async-start | bytes 1474560 | tf_op jit(solution)/shard_map/all_gather | solution.py:72
  260.5 2.5 copy-start.2
  276.6 2.9 copy-start
  279.4 5.7 %copy-start.7 = (f32[4,192]{1,0:T(4,128)S(1)}, f32[4,192]{1,0:T(4,128)}, u32[]{:S(2)}) copy-start(f32[4,192]{1,0:T(4,128)} %param.21) | copy-start | bytes 9220
  279.5 5.7 %copy-start.8 = (f32[4,192]{1,0:T(4,128)S(1)}, f32[4,192]{1,0:T(4,128)}, u32[]{:S(2)}) copy-start(f32[4,192]{1,0:T(4,128)} %param.22) | copy-start | bytes 9220
  279.5 5.7 %copy-start.9 = (f32[4,192]{1,0:T(4,128)S(1)}, f32[4,192]{1,0:T(4,128)}, u32[]{:S(2)}) copy-start(f32[4,192]{1,0:T(4,128)} %param.23) | copy-start | bytes 9220
  279.5 94.9 %all-gather.4.cloned.1.call-start = ((), (), s32[]{:S(2)}) async-start(), calls=%async_computation.5 | async-start | bytes 3932160 | tf_op jit(solution)/shard_map/all_gather | solution.py:71
  374.3 3.9 copy-start.3
Sparse Core Ops, SparseCore 0:
  10.9 49.9 reduce-scatter.7
  63.2 110.4 reduce-scatter.5
  176.5 19.7 reduce-scatter.9
  199.9 60.5 all-reduce.2
  279.6 29.6 all-gather.5
  311.3 62.9 all-gather.3
where the time goes:
time: 387 us; the launch traced here: 386 us
  waiting for transfers between devices  309 us (80%)
  blocking collectives  33.2 us (9%)
  other arithmetic  18.9 us (5%)
  between operations  16.9 us (4%)
  local copies, waits for them, and re-layouts  8.12 us (2%)
    reduce_scatter x1, waiting for transfers between devices, shards(): lax.psum_scatter(embed_term, 'shard', scatter_dimension=0, tiled=True)  113 us
    all_gather x1, waiting for transfers between devices, shards(): lax.all_gather(embed_out[3], 'shard', axis=0, tiled=True)  65.1 us
    psum x1, waiting for transfers between devices, shards(): lax.psum((embed_sum, proj_sum, norm_sum), 'rep')  49.4 us
    reduce_scatter x1, waiting for transfers between devices, shards(): lax.psum_scatter(proj_term, 'shard', scatter_dimension=0, tiled=True)  45.7 us
    unnamed x7, waiting for transfers between devices  22.7 us
    psum x1, blocking collectives, shards(): lax.psum((embed_sum, proj_sum, norm_sum), 'rep')  13.2 us
    all_gather x1, waiting for transfers between devices, shards(): lax.all_gather(proj_out[3], 'shard', axis=0, tiled=True)  13 us
    psum x1, blocking collectives, shards(): squares = lax.psum(square_sum(embed_sum, proj_sum, norm_sum), 'shard')  10.2 us
  transfers between devices with their start and end apart: 6, of which 6 were waited for; matrix products, arithmetic and copies ran while one was open for 3% of the time, Pallas kernels for 0%

commit v1 on v0

v1 whole, which is shorter than its diff:
```python
import functools

import jax
import jax.numpy as jnp
from jax import lax
from jax.experimental import pallas as pl
from jax.experimental.pallas import tpu as pltpu
from jax.sharding import PartitionSpec as P

beta_one = 0.9
beta_two = 0.95
adam_step = 10.0
adam_eps = 1e-08
learning_rate = 0.002
clip_rms = 1.0
LANES = 128
MESH = pl.DeviceIdType.MESH


def adamw(gradient, master, first, second, weight_decay):
    corr_one = 1.0 - beta_one**adam_step
    corr_two = 1.0 - beta_two**adam_step
    first_new = beta_one * first + (1.0 - beta_one) * gradient
    second_new = beta_two * second + (1.0 - beta_two) * gradient * gradient
    direction = (
        first_new / corr_one / (jnp.sqrt(second_new / corr_two) + adam_eps) + weight_decay * master
    )
    master_new = master - learning_rate * direction
    return (master_new, first_new, second_new)


def bit_of(index, bit):
    return lax.rem(lax.div(index, 1 << bit), 2)


def flipped(index, mask):
    bit = 0
    out = index
    while mask >> bit:
        if (mask >> bit) & 1:
            out = out + (1 - 2 * bit_of(index, bit)) * (1 << bit)
        bit += 1
    return out


def tile_sum(values):
    return jnp.sum(values.reshape(values.shape[0] // 8, 8, LANES), axis=0)


def kernel(
    plan,
    grad_embed, grad_proj, grad_norm,
    embed_m, embed_f, embed_s, proj_m, proj_f, proj_s, norm_m, norm_f, norm_s,
    out_em, out_ef, out_es, out_ew, out_pm, out_pf, out_ps, out_pw,
    out_nm, out_nf, out_ns, out_nw,
    own_e, own_p, got_e, got_p, work, sums,
    state_em, state_ef, state_es, state_pm, state_pf, state_ps, local_ew, local_pw,
    norm_acc, norm_got, norm_w, square_acc, square_got, factor_ref,
    *rest,
):
    reps, shards, chunks, e_half, p_half, half_rows, entry_count = plan
    send_sem, recv_sem, local_sem = rest[-3:]
    landed = rest[:-3]
    rep_bits = reps.bit_length() - 1
    shard_bits = shards.bit_length() - 1
    subs = reps // 2
    block = half_rows // subs
    piece = e_half // subs
    rep = lax.axis_index("rep")
    shard = lax.axis_index("shard")
    core = lax.rem(rep, 2)
    sub = lax.div(rep, 2)
    where = {"rep": rep, "shard": shard}
    all_bits = [("rep", b) for b in range(rep_bits)] + [("shard", b) for b in range(shard_bits)]

    sends = []
    locals_ = []

    def send(src, dst, axis, bit):
        i = len(sends)
        copy = pltpu.make_async_remote_copy(
            src_ref=src, dst_ref=dst, send_sem=send_sem.at[i], recv_sem=recv_sem.at[i],
            device_id={axis: flipped(where[axis], 1 << bit)}, device_id_type=MESH,
        )
        copy.start()
        sends.append(copy)
        return copy

    def local(src, dst):
        copy = pltpu.make_async_copy(src, dst, local_sem.at[len(locals_)])
        copy.start()
        locals_.append(copy)
        return copy

    ascending = list(range(1, rep_bits))
    half_chunks = max(chunks // 2, 1)

    def rep_order(c):
        return ascending if c < half_chunks else ascending[::-1]

    turn = []
    for i in range(half_chunks):
        turn += [c for c in (i, i + half_chunks) if c < chunks]

    own = {}
    for c in turn:
        cols = pl.ds(c * LANES, LANES)
        own[c] = (
            local(grad_embed.at[:, core, :, cols], own_e.at[c]),
            local(grad_proj.at[:, core, :, cols], own_p.at[c]),
        )
    barrier = pltpu.get_barrier_semaphore()
    for axis, b in all_bits:
        pl.semaphore_signal(
            barrier, inc=1, device_id={axis: flipped(where[axis], 1 << b)}, device_id_type=MESH
        )
    pl.semaphore_wait(barrier, len(all_bits))

    other = 1 - core
    first_hop = {}
    for c in turn:
        cols = pl.ds(c * LANES, LANES)
        first_hop[c] = (
            send(grad_embed.at[:, other, :, cols], got_e.at[c], "rep", 0),
            send(grad_proj.at[:, other, :, cols], got_p.at[c], "rep", 0),
        )
    states = [
        local(src, dst)
        for src, dst in (
            (embed_m, state_em), (embed_f, state_ef), (embed_s, state_es),
            (proj_m, state_pm), (proj_f, state_pf), (proj_s, state_ps),
        )
    ]

    norm_acc[0] = grad_norm[...].astype(jnp.float32)
    norm_copy = send(norm_acc.at[0], norm_got.at[0], *all_bits[0])
    norm_round = 0

    dims = [("shard", b) for b in reversed(range(shard_bits))]
    dims += [("rep", b) for b in reversed(range(1, rep_bits))]

    def region(c, done, dim=None, value=None):
        index = [c]
        for d in dims:
            if d == dim:
                index.append(value)
            elif d in done:
                index.append(bit_of(where[d[0]], d[1]))
            else:
                index.append(slice(None))
        return tuple(index)

    def stage_order(c):
        return [("rep", b) for b in rep_order(c)] + [("shard", b) for b in range(shard_bits)]

    hops = {}

    def start_hop(c, k):
        order = stage_order(c)
        dim = order[k]
        theirs = 1 - bit_of(where[dim[0]], dim[1])
        hops[c] = send(work.at[region(c, order[:k], dim, theirs)], landed[k].at[c], *dim)

    for c in turn:
        for copy in own[c]:
            copy.wait()
        for copy in first_hop[c]:
            copy.wait_recv()
        for s in range(shards):
            parts = [
                own_e[c, s].astype(jnp.float32) + got_e[c, s].astype(jnp.float32),
                own_p[c, s].astype(jnp.float32) + got_p[c, s].astype(jnp.float32),
            ]
            pad = half_rows - e_half - p_half
            if pad:
                parts.append(jnp.zeros((pad, LANES), jnp.float32))
            slab = jnp.concatenate(parts, axis=0)
            index = (c,) + tuple((s >> b) & 1 for b in reversed(range(shard_bits)))
            work[index] = slab.reshape((2,) * (rep_bits - 1) + (block, LANES))
        start_hop(c, 0)

    gathers = {}
    masks_of = {c: [0] for c in turn}

    def sub_rows(mask):
        return pl.ds(pl.multiple_of(flipped(sub, mask) * block, 8), block)

    def start_gather(c, t):
        order = rep_order(c)[::-1]
        gathers[c] = []
        if t < len(order):
            for mask in masks_of[c]:
                ref = sums.at[c, core, sub_rows(mask)]
                gathers[c].append(send(ref, ref, "rep", order[t]))
            masks_of[c] = masks_of[c] + [m | 1 << (order[t] - 1) for m in masks_of[c]]
        else:
            ref = sums.at[c, core]
            gathers[c].append(send(ref, ref, "rep", 0))

    def advance_norm(current):
        copy, done = current
        if copy is None:
            return current
        copy.wait_recv()
        norm_acc[done + 1] = norm_acc[done] + norm_got[done]
        done += 1
        if done < len(all_bits):
            return send(norm_acc.at[done], norm_got.at[done], *all_bits[done]), done
        return None, done

    current = (norm_copy, 0)
    squares = jnp.zeros((8, LANES), jnp.float32)
    for k in range(len(dims)):
        for c in turn:
            order = stage_order(c)
            dim = order[k]
            hops[c].wait_recv()
            index = region(c, order[:k], dim, bit_of(where[dim[0]], dim[1]))
            total = work[index] + landed[k][c]
            if k + 1 < len(dims):
                work[index] = total
                start_hop(c, k + 1)
            else:
                sums[c, core, sub_rows(0), :] = total
                squares = squares + tile_sum(total * total)
                start_gather(c, 0)
        current = advance_norm(current)
    while current[0] is not None:
        current = advance_norm(current)

    square_acc[0] = squares
    square_copy = send(square_acc.at[0], square_got.at[0], *all_bits[0])
    rounds = 0

    def advance_square(copy, done):
        copy.wait_recv()
        square_acc[done + 1] = square_acc[done] + square_got[done]
        done += 1
        if done < len(all_bits):
            return send(square_acc.at[done], square_got.at[done], *all_bits[done]), done
        return None, done

    for t in range(1, rep_bits):
        for c in turn:
            for copy in gathers[c]:
                copy.wait_recv()
            start_gather(c, t)
        if square_copy is not None:
            square_copy, rounds = advance_square(square_copy, rounds)
    while square_copy is not None:
        square_copy, rounds = advance_square(square_copy, rounds)
    for c in turn:
        for copy in gathers[c]:
            copy.wait_recv()

    norm_sum = norm_acc[len(all_bits)]
    total = jnp.sum(square_acc[len(all_bits)], axis=(0, 1), keepdims=True)
    total = total + jnp.sum(norm_sum * norm_sum, axis=(0, 1), keepdims=True)
    rms = jnp.sqrt(total / entry_count)
    factor = jnp.minimum(jnp.float32(1.0), clip_rms / (rms + 1e-06))
    factor_ref[...] = jnp.broadcast_to(factor, factor_ref.shape)
    for copy in states:
        copy.wait()

    def update(refs, weights, half, base, core_index):
        rows = 32 if half % 32 == 0 else 16
        m_ref, f_ref, s_ref = refs

        def step(i, carry):
            clip = factor_ref[0:1, :]
            at = pl.ds(pl.multiple_of(core_index * half + i * rows, rows), rows)
            for c in range(chunks):
                cols = pl.ds(c * LANES, LANES)
                grad = clip * sums[c, core_index, pl.ds(pl.multiple_of(base + i * rows, 8), rows), :]
                m, f, s = adamw(grad, m_ref[at, cols], f_ref[at, cols], s_ref[at, cols], 0.01)
                m_ref[at, cols] = m
                f_ref[at, cols] = f
                s_ref[at, cols] = s
                weights[at, cols] = m.astype(jnp.bfloat16)
            return carry

        lax.fori_loop(0, half // rows, step, 0)

    for core_index in range(2):
        update((state_em, state_ef, state_es), local_ew, e_half, 0, core_index)
    norm_cols = norm_m.shape[1]
    mine = norm_acc[len(all_bits), :, 0:norm_cols]
    for s in range(1, shards):
        mine = jnp.where(shard == s, norm_acc[len(all_bits), :, s * norm_cols:(s + 1) * norm_cols], mine)
    m, f, s = adamw(factor_ref[0:1, 0:1] * mine, norm_m[...], norm_f[...], norm_s[...], 0.0)
    out_nm[...] = m
    out_nf[...] = f
    out_ns[...] = s
    norm_w[shard] = m

    width = half_chunks * LANES
    streams = [(0, width, ascending)]
    if width < chunks * LANES:
        streams.append((width, chunks * LANES - width, ascending[::-1]))

    def e_rows(zmask, mask):
        start = flipped(shard, zmask) * (2 * e_half) + core * e_half + flipped(sub, mask) * piece
        return pl.ds(pl.multiple_of(start, 16), piece)

    def e_half_rows(zmask):
        start = flipped(shard, zmask) * (2 * e_half) + core * e_half
        return pl.ds(pl.multiple_of(start, 16), e_half)

    def p_rows(zmask):
        start = flipped(shard, zmask) * (2 * p_half) + core * p_half
        return pl.ds(pl.multiple_of(start, 16), p_half)

    def send_e(zmask, lo, size, bit):
        cols = pl.ds(lo, size)
        if zmask == 0:
            at = pl.ds(pl.multiple_of(core * e_half + sub * piece, 16), piece)
            src = local_ew.at[at, cols]
        else:
            src = out_ew.at[e_rows(zmask, 0), cols]
        return send(src, out_ew.at[e_rows(zmask, 0), cols], "shard", bit)

    def send_p(zmask, bit):
        if zmask == 0:
            src = local_pw.at[pl.ds(pl.multiple_of(core * p_half, 16), p_half)]
        else:
            src = out_pw.at[p_rows(zmask)]
        return send(src, out_pw.at[p_rows(zmask)], "shard", bit)

    def send_n(zmask, bit):
        ref = norm_w.at[flipped(shard, zmask)]
        return send(ref, ref, "shard", bit)

    bits = list(reversed(range(shard_bits)))
    held = [0]
    pending = [[send_e(0, lo, size, bits[0])] for lo, size, _ in streams]
    for core_index in range(2):
        update((state_pm, state_pf, state_ps), local_pw, p_half, e_half, core_index)
    outs = [
        local(src, dst)
        for src, dst in (
            (local_ew, out_ew.at[pl.ds(pl.multiple_of(shard * (2 * e_half), 16), 2 * e_half)]),
            (local_pw, out_pw.at[pl.ds(pl.multiple_of(shard * (2 * p_half), 16), 2 * p_half)]),
            (state_em, out_em), (state_ef, out_ef), (state_es, out_es),
            (state_pm, out_pm), (state_pf, out_pf), (state_ps, out_ps),
        )
    ]
    proj_pending = [send_p(0, bits[0])]
    norm_pending = [send_n(0, bits[0])]
    held = [0, 1 << bits[0]]
    for b in bits[1:]:
        for i, (lo, size, _) in enumerate(streams):
            for copy in pending[i]:
                copy.wait_recv()
            pending[i] = [send_e(z, lo, size, b) for z in held]
        for copy in proj_pending + norm_pending:
            copy.wait_recv()
        proj_pending = [send_p(z, b) for z in held]
        norm_pending = [send_n(z, b) for z in held]
        held = held + [z | 1 << b for z in held]

    masks = [[0] for _ in streams]
    for t in range(rep_bits - 1):
        for i, (lo, size, order) in enumerate(streams):
            for copy in pending[i]:
                copy.wait_recv()
            pending[i] = []
            for m in masks[i]:
                for z in range(1, shards):
                    ref = out_ew.at[e_rows(z, m), pl.ds(lo, size)]
                    pending[i].append(send(ref, ref, "rep", order[t]))
            masks[i] = masks[i] + [m | 1 << (order[t] - 1) for m in masks[i]]
    for copy in proj_pending + norm_pending:
        copy.wait_recv()
    last = []
    for z in range(1, shards):
        ref = out_pw.at[p_rows(z)]
        last.append(send(ref, ref, "rep", 0))
    for i, (lo, size, _) in enumerate(streams):
        for copy in pending[i]:
            copy.wait_recv()
        for z in range(1, shards):
            ref = out_ew.at[e_half_rows(z), pl.ds(lo, size)]
            last.append(send(ref, ref, "rep", 0))
    out_nw[...] = norm_w[...]
    for copy in last:
        copy.wait_recv()
    for copy in sends:
        copy.wait_send()
    for copy in outs:
        copy.wait()


def shards_fn(
    reps,
    shards,
    grad_embed, grad_proj, grad_norms,
    embed_master, embed_first, embed_second,
    proj_master, proj_first, proj_second,
    norm_master, norm_first, norm_second,
):
    embed_rows, width = grad_embed.shape[2:]
    proj_rows = grad_proj.shape[2]
    norm_rows, norm_cols = norm_master.shape
    chunks = width // LANES
    e_half = embed_rows // shards // 2
    p_half = proj_rows // shards // 2
    subs = reps // 2
    unit = 8 * subs
    half_rows = -(-(e_half + p_half) // unit) * unit
    block = half_rows // subs
    entry_count = float((embed_rows + proj_rows + norm_rows) * width)
    rep_bits = reps.bit_length() - 1
    shard_bits = shards.bit_length() - 1
    all_bits = rep_bits + shard_bits
    n_dims = all_bits - 1
    f32, bf16 = jnp.float32, jnp.bfloat16
    n_streams = 2 if chunks > 1 else 1
    copies = 2 * chunks + 2 * all_bits + chunks * n_dims + chunks * subs
    copies += (n_streams + 2) * (shards - 1)
    copies += n_streams * (shards - 1) * subs + (shards - 1)
    plan = (reps, shards, chunks, e_half, p_half, half_rows, entry_count)
    any_spec = pl.BlockSpec(memory_space=pl.ANY)
    vmem_spec = pl.BlockSpec(memory_space=pltpu.VMEM)
    e_part, p_part = (2 * e_half, width), (2 * p_half, width)
    landed = [
        pltpu.VMEM((chunks,) + (2,) * (n_dims - 1 - k) + (block, LANES), f32) for k in range(n_dims)
    ]
    outs = pl.pallas_call(
        functools.partial(kernel, plan),
        out_shape=(
            [jax.ShapeDtypeStruct(e_part, f32)] * 3
            + [jax.ShapeDtypeStruct((embed_rows, width), bf16)]
            + [jax.ShapeDtypeStruct(p_part, f32)] * 3
            + [jax.ShapeDtypeStruct((proj_rows, width), bf16)]
            + [jax.ShapeDtypeStruct((norm_rows, norm_cols), f32)] * 3
            + [jax.ShapeDtypeStruct((shards, norm_rows, norm_cols), f32)]
        ),
        in_specs=[any_spec] * 2 + [vmem_spec] + [any_spec] * 6 + [vmem_spec] * 3,
        out_specs=[any_spec] * 8 + [vmem_spec] * 4,
        scratch_shapes=[
            pltpu.VMEM((chunks, shards, e_half, LANES), bf16),
            pltpu.VMEM((chunks, shards, p_half, LANES), bf16),
            pltpu.VMEM((chunks, shards, e_half, LANES), bf16),
            pltpu.VMEM((chunks, shards, p_half, LANES), bf16),
            pltpu.VMEM((chunks,) + (2,) * n_dims + (block, LANES), f32),
            pltpu.VMEM((chunks, 2, half_rows, LANES), f32),
            pltpu.VMEM(e_part, f32), pltpu.VMEM(e_part, f32), pltpu.VMEM(e_part, f32),
            pltpu.VMEM(p_part, f32), pltpu.VMEM(p_part, f32), pltpu.VMEM(p_part, f32),
            pltpu.VMEM(e_part, bf16), pltpu.VMEM(p_part, bf16),
            pltpu.VMEM((all_bits + 1, norm_rows, width), f32),
            pltpu.VMEM((all_bits, norm_rows, width), f32),
            pltpu.VMEM((shards, norm_rows, norm_cols), f32),
            pltpu.VMEM((all_bits + 1, 8, LANES), f32),
            pltpu.VMEM((all_bits, 8, LANES), f32),
            pltpu.VMEM((8, LANES), f32),
        ]
        + landed
        + [
            pltpu.SemaphoreType.DMA((copies,)),
            pltpu.SemaphoreType.DMA((copies,)),
            pltpu.SemaphoreType.DMA((2 * chunks + 14,)),
        ],
        compiler_params=pltpu.CompilerParams(
            collective_id=0, has_side_effects=True, vmem_limit_bytes=58 * 1024 * 1024
        ),
    )(
        grad_embed.reshape(shards, 2, e_half, width),
        grad_proj.reshape(shards, 2, p_half, width),
        grad_norms[0, 0],
        embed_master, embed_first, embed_second,
        proj_master, proj_first, proj_second,
        norm_master, norm_first, norm_second,
    )
    norm_weights = outs[11].astype(bf16).transpose(1, 0, 2).reshape(norm_rows, width)
    return tuple(outs[:11]) + (norm_weights,)


def solution(mesh):
    grad, part, whole = P("rep", "shard", None, None), P("shard", None), P()
    cols = P(None, "shard")
    return jax.shard_map(
        functools.partial(shards_fn, mesh.shape["rep"], mesh.shape["shard"]),
        mesh=mesh,
        in_specs=(grad,) * 3 + (part,) * 6 + (cols,) * 3,
        out_specs=(part,) * 3 + (whole,) + (part,) * 3 + (whole,) + (cols,) * 3 + (whole,),
        check_vma=False,
    )
```

time: 387 us -> 123 us (0.32)
  waiting for transfers between devices: 309 us -> 0 us
  Pallas kernels: 0 us -> 106 us
  blocking collectives: 33.2 us -> 0 us
  other arithmetic: 18.9 us -> 0.72 us
  between operations: 16.9 us -> 0.68 us
  local copies, waits for them, and re-layouts: 8.12 us -> 14.8 us
    reduce_scatter x2 -> x0, waiting for transfers between devices: 158 us -> none  [the longest x1 113 us: shards(): lax.psum_scatter(embed_term, 'shard', scatter_dimension=0, tiled=True)]
    pallas_call x0 -> x1, Pallas kernels: none -> 106 us  [shards_fn(): pl.pallas_call(functools.partial(kernel, plan), out_shape=[jax.ShapeDtype...]
    all_gather x2 -> x0, waiting for transfers between devices: 78.1 us -> none  [the longest x1 65.1 us: shards(): lax.all_gather(embed_out[3], 'shard', axis=0, tiled=True)]
    psum x1 -> x0, waiting for transfers between devices: 49.4 us -> none  [shards(): lax.psum((embed_sum, proj_sum, norm_sum), 'rep')]
    psum x2 -> x0, blocking collectives: 23.4 us -> none  [the longest x1 13.2 us: shards(): lax.psum((embed_sum, proj_sum, norm_sum), 'rep')]
    unnamed x7 -> x0, waiting for transfers between devices: 22.7 us -> none
    convert_element_type x5 -> x0, other arithmetic: 14.5 us -> none  [the longest x2 8.34 us: adamw(): return (master_new, first_new, second_new, master_new.astype(jnp.bfloat16))]
    all_gather x1 -> x0, blocking collectives: 9.8 us -> none  [shards(): lax.all_gather(norm_out[3], 'shard', axis=1, tiled=True)]
  transfers between devices with their start and end apart: 6 -> 0, of which waited for: 6 -> 0; matrix products, arithmetic and copies ran while one was open for 3% -> 0% of each run, Pallas kernels for 0% -> 0%
where the time goes in v1:
time: 123 us; the launch traced here: 122 us
  Pallas kernels  106 us (86%)
  local copies, waits for them, and re-layouts  14.8 us (12%)
    pallas_call x1, Pallas kernels, shards_fn(): pl.pallas_call(functools.partial(kernel, plan), out_shape=[jax.ShapeDtype...  106 us
    unnamed x31, local copies, waits for them, and re-layouts  14.1 us

profile of v1, /device:TPU:1, one launch (start us, length us, event | category | flops | bytes accessed | tf_op | source)
XLA Modules:
  0.0 122.3 jit_solution(12117771333869089130)
XLA Ops:
  0.6 106.0 %shard_map.211 = (f32[512,768]{1,0:T(8,128)}, f32[512,768]{1,0:T(8,128)}, f32[512,768]{1,0:T(8,128)}, bf16[2048,768]{1,0:T(8,128)(2,1)}, f32[192,768]{1,0:T(8,12...) custom-call(bf16[4,2,256,768]{3,2,1,0:T(8,128)(2,1)} %bitcast.5, ...), custom_call_target="tpu_custom_call" | custom-call | tf_op jit(solution)/shard_map/pallas_call | solution.py:428
  106.7 0.7 convert_bitcast_fusion
  107.4 0.7 reshape.35
  108.1 0.0 copy-start.2
  108.1 2.8 %copy.36 = f32[512,768]{1,0:T(8,128)} copy(f32[512,768]{1,0:T(8,128)} %get-tuple-element.48) | data formatting | bytes 3145728
  110.9 0.0 copy-done.2
  110.9 0.0 copy-start.1
  110.9 1.1 copy.37
  112.0 0.8 copy-done.1
  112.9 0.0 copy-start
  112.9 1.1 copy.38
  114.0 1.3 %copy-done = bf16[2048,768]{1,0:T(8,128)(2,1)S(1)} copy-done((bf16[2048,768]{1,0:T(8,128)(2,1)S(1)}, bf16[2048,768]{1,0:T(8,128)(2,1)}, u32[]{:S(2)}) %copy-start) | copy-done | bytes 3145752
  115.3 0.0 copy-start.6
  115.3 0.0 copy-start.5
  115.3 1.7 %copy.39 = bf16[2048,768]{1,0:T(8,128)(2,1)} copy(bf16[2048,768]{1,0:T(8,128)(2,1)S(1)} %copy-done) | data formatting | bytes 6291456
  117.0 0.0 copy-done.6
  117.0 0.0 copy-start.4
  117.0 0.0 copy-start.3
  117.0 0.8 copy.40
  117.8 0.0 copy-done.5
  117.8 0.8 copy.41
  118.6 0.0 copy-done.4
  118.6 0.0 copy-start.9
  118.6 0.0 copy-start.8
  118.6 0.0 copy-start.7
  118.6 0.8 copy.42
  119.5 0.0 copy-done.3
  119.5 1.0 copy.43
  120.5 0.0 copy-done.9
  120.5 0.6 copy.44
  121.1 0.0 copy-done.8
  121.1 0.6 copy.45
  121.7 0.0 copy-done.7
  121.7 0.6 copy.46
  (1 shorter events, 0.0 us)
Async XLA Ops:
  108.1 2.8 %copy-start.2 = (f32[512,768]{1,0:T(8,128)S(1)}, f32[512,768]{1,0:T(8,128)}, u32[]{:S(2)}) copy-start(f32[512,768]{1,0:T(8,128)} %get-tuple-element.49) | copy-start | bytes 4718596
  110.9 2.0 %copy-start.1 = (f32[512,768]{1,0:T(8,128)S(1)}, f32[512,768]{1,0:T(8,128)}, u32[]{:S(2)}) copy-start(f32[512,768]{1,0:T(8,128)} %get-tuple-element.50) | copy-start | bytes 4718596
  112.9 2.5 %copy-start = (bf16[2048,768]{1,0:T(8,128)(2,1)S(1)}, bf16[2048,768]{1,0:T(8,128)(2,1)}, u32[]{:S(2)}) copy-start(bf16[2048,768]{1,0:T(8,128)(2,1)} %get-tuple-element.51) | copy-start | bytes 9437188
  115.3 1.7 %copy-start.6 = (f32[192,768]{1,0:T(8,128)S(1)}, f32[192,768]{1,0:T(8,128)}, u32[]{:S(2)}) copy-start(f32[192,768]{1,0:T(8,128)} %get-tuple-element.52) | copy-start | bytes 1769476
  115.3 2.5 %copy-start.5 = (f32[192,768]{1,0:T(8,128)S(1)}, f32[192,768]{1,0:T(8,128)}, u32[]{:S(2)}) copy-start(f32[192,768]{1,0:T(8,128)} %get-tuple-element.53) | copy-start | bytes 1769476
  117.0 1.6 %copy-start.4 = (f32[192,768]{1,0:T(8,128)S(1)}, f32[192,768]{1,0:T(8,128)}, u32[]{:S(2)}) copy-start(f32[192,768]{1,0:T(8,128)} %get-tuple-element.54) | copy-start | bytes 1769476
  117.0 2.5 %copy-start.3 = (bf16[768,768]{1,0:T(8,128)(2,1)S(1)}, bf16[768,768]{1,0:T(8,128)(2,1)}, u32[]{:S(2)}) copy-start(bf16[768,768]{1,0:T(8,128)(2,1)} %get-tuple-element.55) | copy-start | bytes 3538948
  118.6 1.8 %copy-start.9 = (f32[4,192]{1,0:T(4,128)S(1)}, f32[4,192]{1,0:T(4,128)}, u32[]{:S(2)}) copy-start(f32[4,192]{1,0:T(4,128)} %get-tuple-element.56) | copy-start | bytes 9220
  118.6 2.4 %copy-start.8 = (f32[4,192]{1,0:T(4,128)S(1)}, f32[4,192]{1,0:T(4,128)}, u32[]{:S(2)}) copy-start(f32[4,192]{1,0:T(4,128)} %get-tuple-element.57) | copy-start | bytes 9220
  118.6 3.0 %copy-start.7 = (f32[4,192]{1,0:T(4,128)S(1)}, f32[4,192]{1,0:T(4,128)}, u32[]{:S(2)}) copy-start(f32[4,192]{1,0:T(4,128)} %get-tuple-element.58) | copy-start | bytes 9220

commit v2 on v1

--- a/solution.py
+++ b/solution.py
@@ -23,7 +23,8 @@
     first_new = beta_one * first + (1.0 - beta_one) * gradient
     second_new = beta_two * second + (1.0 - beta_two) * gradient * gradient
     direction = (
-        first_new / corr_one / (jnp.sqrt(second_new / corr_two) + adam_eps) + weight_decay * master
+        first_new * (1.0 / corr_one) / (jnp.sqrt(second_new * (1.0 / corr_two)) + adam_eps)
+        + weight_decay * master
     )
     master_new = master - learning_rate * direction
     return (master_new, first_new, second_new)
@@ -151,7 +152,10 @@
         return tuple(index)
 
     def stage_order(c):
-        return [("rep", b) for b in rep_order(c)] + [("shard", b) for b in range(shard_bits)]
+        reps_part = [("rep", b) for b in rep_order(c)]
+        first = len(reps_part) if c % half_chunks == half_chunks - 1 else 1
+        shard_part = [("shard", b) for b in range(shard_bits)]
+        return reps_part[:first] + shard_part + reps_part[first:]
 
     hops = {}
 
@@ -208,31 +212,10 @@
             return send(norm_acc.at[done], norm_got.at[done], *all_bits[done]), done
         return None, done
 
-    current = (norm_copy, 0)
-    squares = jnp.zeros((8, LANES), jnp.float32)
-    for k in range(len(dims)):
-        for c in turn:
-            order = stage_order(c)
-            dim = order[k]
-            hops[c].wait_recv()
-            index = region(c, order[:k], dim, bit_of(where[dim[0]], dim[1]))
-            total = work[index] + landed[k][c]
-            if k + 1 < len(dims):
-                work[index] = total
-                start_hop(c, k + 1)
-            else:
-                sums[c, core, sub_rows(0), :] = total
-                squares = squares + tile_sum(total * total)
-                start_gather(c, 0)
-        current = advance_norm(current)
-    while current[0] is not None:
-        current = advance_norm(current)
-
-    square_acc[0] = squares
-    square_copy = send(square_acc.at[0], square_got.at[0], *all_bits[0])
-    rounds = 0
-
-    def advance_square(copy, done):
+    def advance_square(current):
+        copy, done = current
+        if copy is None:
+            return current
         copy.wait_recv()
         square_acc[done + 1] = square_acc[done] + square_got[done]
         done += 1
@@ -240,15 +223,44 @@
             return send(square_acc.at[done], square_got.at[done], *all_bits[done]), done
         return None, done
 
-    for t in range(1, rep_bits):
-        for c in turn:
+    n_dims = len(dims)
+    events = sorted(
+        (1.5 * (c % half_chunks) + k, k, turn.index(c), c)
+        for c in turn for k in range(n_dims + rep_bits - 1)
+    )
+    norm_state, square_state = (norm_copy, 0), (None, 0)
+    squares = jnp.zeros((8, LANES), jnp.float32)
+    reduced = 0
+    for step, (_, k, _, c) in enumerate(events):
+        if k < n_dims:
+            order = stage_order(c)
+            dim = order[k]
+            hops[c].wait_recv()
+            index = region(c, order[:k], dim, bit_of(where[dim[0]], dim[1]))
+            total = work[index] + landed[k][c]
+            if k + 1 < n_dims:
+                work[index] = total
+                start_hop(c, k + 1)
+            else:
+                sums[c, core, sub_rows(0), :] = total
+                start_gather(c, 0)
+                squares = squares + tile_sum(total * total)
+                reduced += 1
+                if reduced == chunks:
+                    square_acc[0] = squares
+                    square_state = (send(square_acc.at[0], square_got.at[0], *all_bits[0]), 0)
+        else:
             for copy in gathers[c]:
                 copy.wait_recv()
-            start_gather(c, t)
-        if square_copy is not None:
-            square_copy, rounds = advance_square(square_copy, rounds)
-    while square_copy is not None:
-        square_copy, rounds = advance_square(square_copy, rounds)
+            start_gather(c, k - n_dims + 1)
+            if reduced == chunks:
+                square_state = advance_square(square_state)
+        if step % 3 == 2:
+            norm_state = advance_norm(norm_state)
+    while norm_state[0] is not None:
+        norm_state = advance_norm(norm_state)
+    while square_state[0] is not None:
+        square_state = advance_square(square_state)
     for c in turn:
         for copy in gathers[c]:
             copy.wait_recv()
@@ -262,16 +274,17 @@
     for copy in states:
         copy.wait()
 
-    def update(refs, weights, half, base, core_index):
-        rows = 32 if half % 32 == 0 else 16
+    def update(refs, weights, half, base, core_index, first, count):
+        rows = 32 if count % 32 == 0 else 16
         m_ref, f_ref, s_ref = refs
 
         def step(i, carry):
             clip = factor_ref[0:1, :]
-            at = pl.ds(pl.multiple_of(core_index * half + i * rows, rows), rows)
+            begin = first + i * rows
+            at = pl.ds(pl.multiple_of(core_index * half + begin, rows), rows)
             for c in range(chunks):
                 cols = pl.ds(c * LANES, LANES)
-                grad = clip * sums[c, core_index, pl.ds(pl.multiple_of(base + i * rows, 8), rows), :]
+                grad = clip * sums[c, core_index, pl.ds(pl.multiple_of(base + begin, 8), rows), :]
                 m, f, s = adamw(grad, m_ref[at, cols], f_ref[at, cols], s_ref[at, cols], 0.01)
                 m_ref[at, cols] = m
                 f_ref[at, cols] = f
@@ -279,10 +292,54 @@
                 weights[at, cols] = m.astype(jnp.bfloat16)
             return carry
 
-        lax.fori_loop(0, half // rows, step, 0)
-
-    for core_index in range(2):
-        update((state_em, state_ef, state_es), local_ew, e_half, 0, core_index)
+        lax.fori_loop(0, count // rows, step, 0)
+
+    def update_e(core_index, first, count):
+        update((state_em, state_ef, state_es), local_ew, e_half, 0, core_index, first, count)
+
+    def update_p(core_index):
+        update((state_pm, state_pf, state_ps), local_pw, p_half, e_half, core_index, 0, p_half)
+
+    width = half_chunks * LANES
+    streams = [(0, width, ascending)]
+    if width < chunks * LANES:
+        streams.append((width, chunks * LANES - width, ascending[::-1]))
+
+    def e_rows(zmask, mask):
+        start = flipped(shard, zmask) * (2 * e_half) + core * e_half + flipped(sub, mask) * piece
+        return pl.ds(pl.multiple_of(start, 16), piece)
+
+    def e_half_rows(zmask):
+        start = flipped(shard, zmask) * (2 * e_half) + core * e_half
+        return pl.ds(pl.multiple_of(start, 16), e_half)
+
+    def p_rows(zmask):
+        start = flipped(shard, zmask) * (2 * p_half) + core * p_half
+        return pl.ds(pl.multiple_of(start, 16), p_half)
+
+    def send_e(zmask, lo, size, bit):
+        cols = pl.ds(lo, size)
+        if zmask == 0:
+            at = pl.ds(pl.multiple_of(core * e_half + sub * piece, 16), piece)
+            src = local_ew.at[at, cols]
+        else:
+            src = out_ew.at[e_rows(zmask, 0), cols]
+        return send(src, out_ew.at[e_rows(zmask, 0), cols], "shard", bit)
+
+    def send_p(zmask, bit):
+        if zmask == 0:
+            src = local_pw.at[pl.ds(pl.multiple_of(core * p_half, 16), p_half)]
+        else:
+            src = out_pw.at[p_rows(zmask)]
+        return send(src, out_pw.at[p_rows(zmask)], "shard", bit)
+
+    def send_n(zmask, bit):
+        ref = norm_w.at[flipped(shard, zmask)]
+        return send(ref, ref, "shard", bit)
+
+    bits = list(reversed(range(shard_bits)))
+    update_e(core, sub * piece, piece)
+    pending = [[send_e(0, lo, size, bits[0])] for lo, size, _ in streams]
     norm_cols = norm_m.shape[1]
     mine = norm_acc[len(all_bits), :, 0:norm_cols]
     for s in range(1, shards):
@@ -292,49 +349,32 @@
     out_nf[...] = f
     out_ns[...] = s
     norm_w[shard] = m
-
-    width = half_chunks * LANES
-    streams = [(0, width, ascending)]
-    if width < chunks * LANES:
-        streams.append((width, chunks * LANES - width, ascending[::-1]))
-
-    def e_rows(zmask, mask):
-        start = flipped(shard, zmask) * (2 * e_half) + core * e_half + flipped(sub, mask) * piece
-        return pl.ds(pl.multiple_of(start, 16), piece)
-
-    def e_half_rows(zmask):
-        start = flipped(shard, zmask) * (2 * e_half) + core * e_half
-        return pl.ds(pl.multiple_of(start, 16), e_half)
-
-    def p_rows(zmask):
-        start = flipped(shard, zmask) * (2 * p_half) + core * p_half
-        return pl.ds(pl.multiple_of(start, 16), p_half)
-
-    def send_e(zmask, lo, size, bit):
-        cols = pl.ds(lo, size)
-        if zmask == 0:
-            at = pl.ds(pl.multiple_of(core * e_half + sub * piece, 16), piece)
-            src = local_ew.at[at, cols]
-        else:
-            src = out_ew.at[e_rows(zmask, 0), cols]
-        return send(src, out_ew.at[e_rows(zmask, 0), cols], "shard", bit)
-
-    def send_p(zmask, bit):
-        if zmask == 0:
-            src = local_pw.at[pl.ds(pl.multiple_of(core * p_half, 16), p_half)]
-        else:
-            src = out_pw.at[p_rows(zmask)]
-        return send(src, out_pw.at[p_rows(zmask)], "shard", bit)
-
-    def send_n(zmask, bit):
-        ref = norm_w.at[flipped(shard, zmask)]
-        return send(ref, ref, "shard", bit)
-
-    bits = list(reversed(range(shard_bits)))
-    held = [0]
-    pending = [[send_e(0, lo, size, bits[0])] for lo, size, _ in streams]
-    for core_index in range(2):
-        update((state_pm, state_pf, state_ps), local_pw, p_half, e_half, core_index)
+    norm_pending = [send_n(0, bits[0])]
+    update_p(core)
+    rest_parts = [functools.partial(update_p, other)]
+    rest_parts += [
+        functools.partial(update_e, core, flipped(sub, m) * piece, piece) for m in range(1, subs)
+    ]
+    rest_parts.append(functools.partial(update_e, other, 0, e_half))
+    rest_parts.reverse()
+    rest_parts.pop(0)()
+    held = [0, 1 << bits[0]]
+    proj_pending = []
+    for n, b in enumerate(bits[1:]):
+        for i, (lo, size, _) in enumerate(streams):
+            for copy in pending[i]:
+                copy.wait_recv()
+            pending[i] = [send_e(z, lo, size, b) for z in held]
+        for copy in norm_pending:
+            copy.wait_recv()
+        norm_pending = [send_n(z, b) for z in held]
+        if n == 0:
+            proj_pending = [send_p(0, bits[0])]
+        held = held + [z | 1 << b for z in held]
+    if not proj_pending:
+        proj_pending = [send_p(0, bits[0])]
+    for part in rest_parts:
+        part()
     outs = [
         local(src, dst)
         for src, dst in (
@@ -344,19 +384,17 @@
             (state_pm, out_pm), (state_pf, out_pf), (state_ps, out_ps),
         )
     ]
-    proj_pending = [send_p(0, bits[0])]
-    norm_pending = [send_n(0, bits[0])]
-    held = [0, 1 << bits[0]]
-    for b in bits[1:]:
-        for i, (lo, size, _) in enumerate(streams):
-            for copy in pending[i]:
+    proj_held = [0, 1 << bits[0]]
+    proj_bits = bits[1:]
+
+    def advance_proj():
+        nonlocal proj_pending, proj_held, proj_bits
+        if proj_bits:
+            b, proj_bits = proj_bits[0], proj_bits[1:]
+            for copy in proj_pending:
                 copy.wait_recv()
-            pending[i] = [send_e(z, lo, size, b) for z in held]
-        for copy in proj_pending + norm_pending:
-            copy.wait_recv()
-        proj_pending = [send_p(z, b) for z in held]
-        norm_pending = [send_n(z, b) for z in held]
-        held = held + [z | 1 << b for z in held]
+            proj_pending = [send_p(z, b) for z in proj_held]
+            proj_held = proj_held + [z | 1 << b for z in proj_held]
 
     masks = [[0] for _ in streams]
     for t in range(rep_bits - 1):
@@ -369,6 +407,9 @@
                     ref = out_ew.at[e_rows(z, m), pl.ds(lo, size)]
                     pending[i].append(send(ref, ref, "rep", order[t]))
             masks[i] = masks[i] + [m | 1 << (order[t] - 1) for m in masks[i]]
+        advance_proj()
+    while proj_bits:
+        advance_proj()
     for copy in proj_pending + norm_pending:
         copy.wait_recv()
     last = []

time: 123 us -> 119 us (0.967)
  Pallas kernels: 106 us -> 102 us
    pallas_call x1, Pallas kernels: 106 us -> 102 us  [shards_fn(): pl.pallas_call(functools.partial(kernel, plan), out_shape=[jax.ShapeDtype...]
where the time goes in v2:
time: 119 us; the launch traced here: 118 us
  Pallas kernels  102 us (86%)
  local copies, waits for them, and re-layouts  14.8 us (12%)
    pallas_call x1, Pallas kernels, shards_fn(): pl.pallas_call(functools.partial(kernel, plan), out_shape=[jax.ShapeDtype...  102 us
    unnamed x31, local copies, waits for them, and re-layouts  14.1 us

profile of v2, /device:TPU:1, one launch (start us, length us, event | category | flops | bytes accessed | tf_op | source)
XLA Modules:
  0.0 118.3 jit_solution(7802747735976465266)
XLA Ops:
  0.6 102.1 %shard_map.211 = (f32[512,768]{1,0:T(8,128)}, f32[512,768]{1,0:T(8,128)}, f32[512,768]{1,0:T(8,128)}, bf16[2048,768]{1,0:T(8,128)(2,1)}, f32[192,768]{1,0:T(8,12...) custom-call(bf16[4,2,256,768]{3,2,1,0:T(8,128)(2,1)} %bitcast.5, ...), custom_call_target="tpu_custom_call" | custom-call | tf_op jit(solution)/shard_map/pallas_call | solution.py:469
  102.8 0.7 convert_bitcast_fusion
  103.5 0.7 reshape.35
  104.2 0.0 copy-start.2
  104.2 2.8 %copy.36 = f32[512,768]{1,0:T(8,128)} copy(f32[512,768]{1,0:T(8,128)} %get-tuple-element.48) | data formatting | bytes 3145728
  106.9 0.0 copy-done.2
  107.0 0.0 copy-start.1
  107.0 1.1 copy.37
  108.1 0.8 copy-done.1
  108.9 0.0 copy-start
  108.9 1.1 copy.38
  110.1 1.3 %copy-done = bf16[2048,768]{1,0:T(8,128)(2,1)S(1)} copy-done((bf16[2048,768]{1,0:T(8,128)(2,1)S(1)}, bf16[2048,768]{1,0:T(8,128)(2,1)}, u32[]{:S(2)}) %copy-start) | copy-done | bytes 3145752
  111.4 0.0 copy-start.6
  111.4 0.0 copy-start.5
  111.4 1.7 %copy.39 = bf16[2048,768]{1,0:T(8,128)(2,1)} copy(bf16[2048,768]{1,0:T(8,128)(2,1)S(1)} %copy-done) | data formatting | bytes 6291456
  113.1 0.0 copy-done.6
  113.1 0.0 copy-start.4
  113.1 0.0 copy-start.3
  113.1 0.8 copy.40
  113.9 0.0 copy-done.5
  113.9 0.8 copy.41
  114.7 0.0 copy-done.4
  114.7 0.0 copy-start.9
  114.7 0.0 copy-start.8
  114.7 0.0 copy-start.7
  114.7 0.8 copy.42
  115.5 0.0 copy-done.3
  115.5 1.0 copy.43
  116.5 0.0 copy-done.9
  116.5 0.6 copy.44
  117.1 0.0 copy-done.8
  117.1 0.6 copy.45
  117.7 0.0 copy-done.7
  117.7 0.6 copy.46
  (1 shorter events, 0.0 us)
Async XLA Ops:
  104.2 2.8 %copy-start.2 = (f32[512,768]{1,0:T(8,128)S(1)}, f32[512,768]{1,0:T(8,128)}, u32[]{:S(2)}) copy-start(f32[512,768]{1,0:T(8,128)} %get-tuple-element.49) | copy-start | bytes 4718596
  107.0 2.0 %copy-start.1 = (f32[512,768]{1,0:T(8,128)S(1)}, f32[512,768]{1,0:T(8,128)}, u32[]{:S(2)}) copy-start(f32[512,768]{1,0:T(8,128)} %get-tuple-element.50) | copy-start | bytes 4718596
  108.9 2.5 %copy-start = (bf16[2048,768]{1,0:T(8,128)(2,1)S(1)}, bf16[2048,768]{1,0:T(8,128)(2,1)}, u32[]{:S(2)}) copy-start(bf16[2048,768]{1,0:T(8,128)(2,1)} %get-tuple-element.51) | copy-start | bytes 9437188
  111.4 1.7 %copy-start.6 = (f32[192,768]{1,0:T(8,128)S(1)}, f32[192,768]{1,0:T(8,128)}, u32[]{:S(2)}) copy-start(f32[192,768]{1,0:T(8,128)} %get-tuple-element.52) | copy-start | bytes 1769476
  111.4 2.5 %copy-start.5 = (f32[192,768]{1,0:T(8,128)S(1)}, f32[192,768]{1,0:T(8,128)}, u32[]{:S(2)}) copy-start(f32[192,768]{1,0:T(8,128)} %get-tuple-element.53) | copy-start | bytes 1769476
  113.1 1.6 %copy-start.4 = (f32[192,768]{1,0:T(8,128)S(1)}, f32[192,768]{1,0:T(8,128)}, u32[]{:S(2)}) copy-start(f32[192,768]{1,0:T(8,128)} %get-tuple-element.54) | copy-start | bytes 1769476
  113.1 2.5 %copy-start.3 = (bf16[768,768]{1,0:T(8,128)(2,1)S(1)}, bf16[768,768]{1,0:T(8,128)(2,1)}, u32[]{:S(2)}) copy-start(bf16[768,768]{1,0:T(8,128)(2,1)} %get-tuple-element.55) | copy-start | bytes 3538948
  114.7 1.8 %copy-start.9 = (f32[4,192]{1,0:T(4,128)S(1)}, f32[4,192]{1,0:T(4,128)}, u32[]{:S(2)}) copy-start(f32[4,192]{1,0:T(4,128)} %get-tuple-element.56) | copy-start | bytes 9220
  114.7 2.4 %copy-start.8 = (f32[4,192]{1,0:T(4,128)S(1)}, f32[4,192]{1,0:T(4,128)}, u32[]{:S(2)}) copy-start(f32[4,192]{1,0:T(4,128)} %get-tuple-element.57) | copy-start | bytes 9220
  114.7 3.0 %copy-start.7 = (f32[4,192]{1,0:T(4,128)S(1)}, f32[4,192]{1,0:T(4,128)}, u32[]{:S(2)}) copy-start(f32[4,192]{1,0:T(4,128)} %get-tuple-element.58) | copy-start | bytes 9220

commit v3 on v2

--- a/solution.py
+++ b/solution.py
@@ -308,10 +308,6 @@
     def e_rows(zmask, mask):
         start = flipped(shard, zmask) * (2 * e_half) + core * e_half + flipped(sub, mask) * piece
         return pl.ds(pl.multiple_of(start, 16), piece)
-
-    def e_half_rows(zmask):
-        start = flipped(shard, zmask) * (2 * e_half) + core * e_half
-        return pl.ds(pl.multiple_of(start, 16), e_half)
 
     def p_rows(zmask):
         start = flipped(shard, zmask) * (2 * p_half) + core * p_half
@@ -397,6 +393,16 @@
             proj_held = proj_held + [z | 1 << b for z in proj_held]
 
     masks = [[0] for _ in streams]
+    fresh = [[0] for _ in streams]
+    last = []
+
+    def send_core(i):
+        lo, size, _ = streams[i]
+        for m in fresh[i]:
+            for z in range(1, shards):
+                ref = out_ew.at[e_rows(z, m), pl.ds(lo, size)]
+                last.append(send(ref, ref, "rep", 0))
+
     for t in range(rep_bits - 1):
         for i, (lo, size, order) in enumerate(streams):
             for copy in pending[i]:
@@ -406,22 +412,21 @@
                 for z in range(1, shards):
                     ref = out_ew.at[e_rows(z, m), pl.ds(lo, size)]
                     pending[i].append(send(ref, ref, "rep", order[t]))
-            masks[i] = masks[i] + [m | 1 << (order[t] - 1) for m in masks[i]]
+            send_core(i)
+            fresh[i] = [m | 1 << (order[t] - 1) for m in masks[i]]
+            masks[i] = masks[i] + fresh[i]
         advance_proj()
     while proj_bits:
         advance_proj()
     for copy in proj_pending + norm_pending:
         copy.wait_recv()
-    last = []
     for z in range(1, shards):
         ref = out_pw.at[p_rows(z)]
         last.append(send(ref, ref, "rep", 0))
     for i, (lo, size, _) in enumerate(streams):
         for copy in pending[i]:
             copy.wait_recv()
-        for z in range(1, shards):
-            ref = out_ew.at[e_half_rows(z), pl.ds(lo, size)]
-            last.append(send(ref, ref, "rep", 0))
+        send_core(i)
     out_nw[...] = norm_w[...]
     for copy in last:
         copy.wait_recv()
@@ -457,7 +462,7 @@
     f32, bf16 = jnp.float32, jnp.bfloat16
     n_streams = 2 if chunks > 1 else 1
     copies = 2 * chunks + 2 * all_bits + chunks * n_dims + chunks * subs
-    copies += (n_streams + 2) * (shards - 1)
+    copies += (n_streams + 2) * (shards - 1) + n_streams * (shards - 1) * subs
     copies += n_streams * (shards - 1) * subs + (shards - 1)
     plan = (reps, shards, chunks, e_half, p_half, half_rows, entry_count)
     any_spec = pl.BlockSpec(memory_space=pl.ANY)

time: 119 us -> 119 us (level)
  no operation moved by 1% of the time
where the time goes in v3:
time: 119 us; the launch traced here: 118 us
  Pallas kernels  102 us (86%)
  local copies, waits for them, and re-layouts  14.8 us (12%)
    pallas_call x1, Pallas kernels, shards_fn(): pl.pallas_call(functools.partial(kernel, plan), out_shape=[jax.ShapeDtype...  102 us
    unnamed x31, local copies, waits for them, and re-layouts  14.1 us

profile of v3, /device:TPU:1, one launch (start us, length us, event | category | flops | bytes accessed | tf_op | source)
XLA Modules:
  0.0 118.4 jit_solution(3288173762245639255)
XLA Ops:
  0.6 102.1 %shard_map.211 = (f32[512,768]{1,0:T(8,128)}, f32[512,768]{1,0:T(8,128)}, f32[512,768]{1,0:T(8,128)}, bf16[2048,768]{1,0:T(8,128)(2,1)}, f32[192,768]{1,0:T(8,12...) custom-call(bf16[4,2,256,768]{3,2,1,0:T(8,128)(2,1)} %bitcast.5, ...), custom_call_target="tpu_custom_call" | custom-call | tf_op jit(solution)/shard_map/pallas_call | solution.py:474
  102.8 0.7 convert_bitcast_fusion
  103.5 0.7 reshape.35
  104.2 0.0 copy-start.2
  104.2 2.8 %copy.36 = f32[512,768]{1,0:T(8,128)} copy(f32[512,768]{1,0:T(8,128)} %get-tuple-element.48) | data formatting | bytes 3145728
  107.0 0.0 copy-done.2
  107.0 0.0 copy-start.1
  107.0 1.1 copy.37
  108.1 0.8 copy-done.1
  109.0 0.0 copy-start
  109.0 1.1 copy.38
  110.1 1.3 %copy-done = bf16[2048,768]{1,0:T(8,128)(2,1)S(1)} copy-done((bf16[2048,768]{1,0:T(8,128)(2,1)S(1)}, bf16[2048,768]{1,0:T(8,128)(2,1)}, u32[]{:S(2)}) %copy-start) | copy-done | bytes 3145752
  111.4 0.0 copy-start.6
  111.4 0.0 copy-start.5
  111.4 1.7 %copy.39 = bf16[2048,768]{1,0:T(8,128)(2,1)} copy(bf16[2048,768]{1,0:T(8,128)(2,1)S(1)} %copy-done) | data formatting | bytes 6291456
  113.1 0.0 copy-done.6
  113.1 0.0 copy-start.4
  113.1 0.0 copy-start.3
  113.1 0.8 copy.40
  113.9 0.0 copy-done.5
  113.9 0.8 copy.41
  114.7 0.0 copy-done.4
  114.7 0.0 copy-start.9
  114.7 0.0 copy-start.8
  114.7 0.0 copy-start.7
  114.7 0.8 copy.42
  115.6 0.0 copy-done.3
  115.6 1.0 copy.43
  116.6 0.0 copy-done.9
  116.6 0.6 copy.44
  117.2 0.0 copy-done.8
  117.2 0.6 copy.45
  117.8 0.0 copy-done.7
  117.8 0.6 copy.46
  (1 shorter events, 0.0 us)
Async XLA Ops:
  104.2 2.8 %copy-start.2 = (f32[512,768]{1,0:T(8,128)S(1)}, f32[512,768]{1,0:T(8,128)}, u32[]{:S(2)}) copy-start(f32[512,768]{1,0:T(8,128)} %get-tuple-element.49) | copy-start | bytes 4718596
  107.0 2.0 %copy-start.1 = (f32[512,768]{1,0:T(8,128)S(1)}, f32[512,768]{1,0:T(8,128)}, u32[]{:S(2)}) copy-start(f32[512,768]{1,0:T(8,128)} %get-tuple-element.50) | copy-start | bytes 4718596
  109.0 2.5 %copy-start = (bf16[2048,768]{1,0:T(8,128)(2,1)S(1)}, bf16[2048,768]{1,0:T(8,128)(2,1)}, u32[]{:S(2)}) copy-start(bf16[2048,768]{1,0:T(8,128)(2,1)} %get-tuple-element.51) | copy-start | bytes 9437188
  111.4 1.7 %copy-start.6 = (f32[192,768]{1,0:T(8,128)S(1)}, f32[192,768]{1,0:T(8,128)}, u32[]{:S(2)}) copy-start(f32[192,768]{1,0:T(8,128)} %get-tuple-element.52) | copy-start | bytes 1769476
  111.4 2.5 %copy-start.5 = (f32[192,768]{1,0:T(8,128)S(1)}, f32[192,768]{1,0:T(8,128)}, u32[]{:S(2)}) copy-start(f32[192,768]{1,0:T(8,128)} %get-tuple-element.53) | copy-start | bytes 1769476
  113.1 1.6 %copy-start.4 = (f32[192,768]{1,0:T(8,128)S(1)}, f32[192,768]{1,0:T(8,128)}, u32[]{:S(2)}) copy-start(f32[192,768]{1,0:T(8,128)} %get-tuple-element.54) | copy-start | bytes 1769476
  113.1 2.5 %copy-start.3 = (bf16[768,768]{1,0:T(8,128)(2,1)S(1)}, bf16[768,768]{1,0:T(8,128)(2,1)}, u32[]{:S(2)}) copy-start(bf16[768,768]{1,0:T(8,128)(2,1)} %get-tuple-element.55) | copy-start | bytes 3538948
  114.7 1.8 %copy-start.9 = (f32[4,192]{1,0:T(4,128)S(1)}, f32[4,192]{1,0:T(4,128)}, u32[]{:S(2)}) copy-start(f32[4,192]{1,0:T(4,128)} %get-tuple-element.56) | copy-start | bytes 9220
  114.7 2.4 %copy-start.8 = (f32[4,192]{1,0:T(4,128)S(1)}, f32[4,192]{1,0:T(4,128)}, u32[]{:S(2)}) copy-start(f32[4,192]{1,0:T(4,128)} %get-tuple-element.57) | copy-start | bytes 9220
  114.7 3.0 %copy-start.7 = (f32[4,192]{1,0:T(4,128)S(1)}, f32[4,192]{1,0:T(4,128)}, u32[]{:S(2)}) copy-start(f32[4,192]{1,0:T(4,128)} %get-tuple-element.58) | copy-start | bytes 9220
